TPU v7x, 32 devices: a whole 2x2x4 slice. The times are simulated.
32 devices in a mesh: row: 8 (over z, x), col: 4 (over y, core).
Axes of the slice: x: 2, y: 2, z: 4, core: 2. Of those that a mesh axis runs over, the one named last changes fastest.
Arguments:
- inverse_block: bfloat16 [10240, 10240], P('row', 'col'), may hold values from -6 to 6
- factor_cols: bfloat16 [10240, 1024], P('row', 'col'), may hold values from -0.078125 to 0.078125
- diag_inverse: float32 [4, 256, 256], P('col', 'row'), may hold values from -6 to 6
- fill_mask: int32 [40, 4], replicated, may hold values from 0 to 1
Outputs:
- inverse_cols: bfloat16 [10240, 1024], P('row', 'col')
- inverse_diag: float32 [4, 256, 256], P('col', 'row')
All inputs are finite; a program needn't handle non-finite values.
Results may differ from a plain program's by a relative error of at most 0.0027.
Values may be sent and summed in bfloat16 or wider, within the bound.
A program may use at most 64 MiB of HBM per device.

v0:
```python
import jax
import jax.numpy as jnp
from jax import lax
from jax.sharding import PartitionSpec as P


def body(inverse_block, factor_cols, diag_inverse, fill_mask):
    rows_device, cols_device = factor_cols.shape
    nodes_device, diag_rows, block_width = diag_inverse.shape
    block_count, node_count = fill_mask.shape
    row_index = lax.axis_index("row")
    col_index = lax.axis_index("col")
    expanded = jnp.broadcast_to(
        fill_mask[:, None, :], (block_count, block_width, node_count)
    ).reshape(block_count * block_width, node_count)
    local_mask = lax.dynamic_slice(
        expanded, (row_index * rows_device, col_index * nodes_device), (rows_device, nodes_device)
    )
    column_mask = jnp.broadcast_to(
        local_mask[:, :, None], (rows_device, nodes_device, block_width)
    ).reshape(rows_device, cols_device)
    selected = factor_cols * column_mask.astype(jnp.bfloat16)
    gathered_panel = lax.all_gather(selected, "row", axis=0, tiled=True)
    spread = lax.all_to_all(gathered_panel, "col", split_axis=0, concat_axis=1, tiled=True)
    partial_value = jnp.dot(inverse_block, spread, preferred_element_type=jnp.float32)
    summed = lax.psum_scatter(partial_value, "col", scatter_dimension=1, tiled=True)
    inverse_cols = (-summed * column_mask.astype(jnp.float32)).astype(jnp.bfloat16)
    left_side = selected.reshape(rows_device, nodes_device, block_width)
    right_side = inverse_cols.reshape(rows_device, nodes_device, block_width)
    correction = jnp.einsum(
        "isa,isb->sab", left_side, right_side, preferred_element_type=jnp.float32
    )
    shared = lax.psum_scatter(correction, "row", scatter_dimension=1, tiled=True)
    inverse_diag = diag_inverse - shared
    return (inverse_cols, inverse_diag)


def solution(mesh):
    placed = (P("row", "col"), P("row", "col"), P("col", "row", None), P())
    return jax.shard_map(
        body,
        mesh=mesh,
        in_specs=placed,
        out_specs=(P("row", "col"), P("col", "row", None)),
        check_vma=False,
    )
```

profile of v0, /device:TPU:1, one launch (start us, length us, event | category | flops | bytes accessed | tf_op | source)
XLA Modules:
  0.0 304.7 jit_solution(8671218205381961027)
XLA Ops:
  7.2 0.0 copy-start
  7.2 0.0 all-gather.2.cloned.1.call-start
  7.2 0.6 copy-done
  7.9 0.1 broadcast_bitcast_fusion
  7.9 0.1 copy.11
  8.0 0.1 convert_reduce_fusion.1
  8.1 2.2 broadcast_multiply_fusion
  10.3 0.0 all-gather.2.cloned.1.call-update
  10.3 0.0 reduce-scatter.3.cloned.1.call-start
  10.4 87.9 %all-gather.2.cloned.1.call-done = bf16[10240,256]{1,0:T(8,128)(2,1)} async-done(((bf16[1280,256]{1,0:T(8,128)(2,1)}), bf16[10240,256]{1,0:T(8,128)(2,1)}) %all-gather.2.cloned.1.call-update) | async-done | bytes 5242896 | tf_op jit(solution)/shard_map/all_gather | solution.py:23
  98.3 66.0 %all_to_all.19 = bf16[4,2560,256]{2,1,0:T(8,128)(2,1)} all-to-all(bf16[4,2560,256]{2,1,0:T(8,128)(2,1)} %bitcast.17), channel_id=1, replica_groups=mesh['row'=8,'col'=4] {'col'}, dimensions={0} | all-to-all | bytes 10485760 | tf_op jit(solution)/shard_map/all_to_all | solution.py:24
  164.3 7.8 %copy.9 = bf16[2560,4,256]{0,2,1:T(8,128)(2,1)} copy(bf16[2560,4,256]{2,0,1:T(8,128)(2,1)} %bitcast.16) | data formatting | bytes 10485760 | tf_op jit(solution)/shard_map/all_to_all | solution.py:24
  172.1 12.3 %convolution_bitcast_fusion = f32[1280,1024]{0,1:T(8,128)} fusion(bf16[2560,1024]{0,1:T(8,128)(2,1)} %bitcast.18, bf16[1280,2560]{1,0:T(8,128)(2,1)} %param.4), kind=kOutput, calls=%fused_computation | convolution fusion | flops 6710886400 | bytes 17039360 | tf_op jit(solution)/shard_map/dot_general | solution.py:25
  184.4 0.0 reduce-scatter.3.cloned.1.call-update
  184.5 0.0 reduce-scatter.5.cloned.1.call-start
  184.5 0.1 convert_reduce_fusion
  184.6 49.1 %reduce-scatter.3.cloned.1.call-done = f32[1280,256]{0,1:T(8,128)} async-done(((f32[1280,1024]{0,1:T(8,128)}), f32[1280,256]{0,1:T(8,128)}) %reduce-scatter.3.cloned.1.call-update) | async-done | bytes 1310736 | tf_op jit(solution)/shard_map/reduce_scatter | solution.py:26
  233.7 1.4 multiply_convert_fusion
  235.1 1.1 convolution_bitcast_fusion.1
  236.2 0.0 reduce-scatter.5.cloned.1.call-update
  236.2 1.1 copy.10
  237.3 59.5 %reduce-scatter.5.cloned.1.call-done = f32[1,32,256]{2,1,0:T(8,128)} async-done(((f32[1,256,256]{2,1,0:T(8,128)}), f32[1,32,256]{2,1,0:T(8,128)}) %reduce-scatter.5.cloned.1.call-update) | async-done | bytes 32784 | tf_op jit(solution)/shard_map/reduce_scatter | solution.py:33
  296.8 0.0 copy-done.2
  296.8 1.4 sub.3
  (3 shorter events, 0.0 us)
Async XLA Ops:
  7.2 0.7 copy-start
  7.2 91.1 %all-gather.2.cloned.1.call-start = ((), (), s32[]{:S(2)}) async-start(), calls=%async_computation.3 | async-start | bytes 5898240 | tf_op jit(solution)/shard_map/all_gather | solution.py:23
  10.3 223.4 %reduce-scatter.3.cloned.1.call-start = ((), (), s32[]{:S(2)}) async-start(), calls=%async_computation.4 | async-start | bytes 6553600 | tf_op jit(solution)/shard_map/reduce_scatter | solution.py:26
  184.4 50.7 %copy-start.1 = (bf16[1280,256]{1,0:T(8,128)(2,1)S(1)}, bf16[1280,256]{1,0:T(8,128)(2,1)}, u32[]{:S(2)}) copy-start(bf16[1280,256]{1,0:T(8,128)(2,1)} %broadcast_multiply_fusion) | copy-start | bytes 1966084
  184.4 112.4 %copy-start.2 = (f32[1,32,256]{2,1,0:T(8,128)S(1)}, f32[1,32,256]{2,1,0:T(8,128)}, u32[]{:S(2)}) copy-start(f32[1,32,256]{2,1,0:T(8,128)} %param.6) | copy-start | bytes 98308
  184.5 112.3 %reduce-scatter.5.cloned.1.call-start = ((), (), s32[]{:S(2)}) async-start(), calls=%async_computation.5 | async-start | bytes 294912 | tf_op jit(solution)/shard_map/reduce_scatter | solution.py:33
Sparse Core Ops, SparseCore 0:
  10.8 87.4 all-gather.1
  184.6 49.0 reduce-scatter.2
  237.4 59.3 reduce-scatter.4
where the time goes:
time: 308 us; the launch traced here: 305 us
  waiting for transfers between devices  197 us (64%)
  blocking collectives  66 us (21%)
  between operations  13.8 us (4%)
  matrix products  13.4 us (4%)
  local copies, waits for them, and re-layouts  9.69 us (3%)
  other arithmetic  5.17 us (2%)
    all_gather x1, waiting for transfers between devices, body(): gathered_panel = lax.all_gather(selected, 'row', axis=0, tiled=True)  87.9 us
    all_to_all x1, blocking collectives, body(): lax.all_to_all(gathered_panel, 'col', split_axis=0, concat_axis=1, tiled=...  66 us
    reduce_scatter x1, waiting for transfers between devices, body(): lax.psum_scatter(correction, 'row', scatter_dimension=1, tiled=True)  59.5 us
    reduce_scatter x1, waiting for transfers between devices, body(): lax.psum_scatter(partial_value, 'col', scatter_dimension=1, tiled=True)  49.1 us
    dot_general x1, matrix products, body(): jnp.dot(inverse_block, spread, preferred_element_type=jnp.float32)  12.3 us
    all_to_all x1, local copies, waits for them, and re-layouts, body(): lax.all_to_all(gathered_panel, 'col', split_axis=0, concat_axis=1, tiled=...  7.83 us
  transfers between devices with their start and end apart: 3, of which 3 were waited for; matrix products, arithmetic and copies ran while one was open for 0% of the time, Pallas kernels for 0%

commit v1 on v0

v1 whole, which is shorter than its diff:
```python
import functools
import math

import jax
import jax.numpy as jnp
from jax import lax
from jax.experimental import pallas as pl
from jax.experimental.pallas import tpu as pltpu
from jax.sharding import PartitionSpec as P

LANES = 128
PARTS = 4
TILES = 4
MESH = pl.DeviceIdType.MESH


def split_rows(extent, most):
    return max(n for n in range(1, most + 1) if extent % n == 0 and (extent // n) % 16 == 0)


def kernel(
    R, C, X, mask_ref, factor_ref, diag_ref, a_hbm, out_ref, diag_out_ref,
    a_ref, zbuf, fbuf, part, pair_recv, ysend, yrecv, corr, corr_recv,
    a_sem, z_send, z_recv, b_send, f_recv, x_send, x_recv,
    p_send, p_recv, y_send, y_recv, c_send, c_recv,
):
    Z, G, M = R // X, R // C, C // 2
    rows, cols = factor_ref.shape
    halves = cols // LANES
    width = diag_ref.shape[-1]
    diag_rows = diag_ref.shape[1]
    parts, tiles = z_recv.shape[1] // halves, p_send.shape[1]
    J = halves * parts
    pr, mt = rows // parts, rows // tiles
    r, c = lax.axis_index("row"), lax.axis_index("col")
    z, x = r // X, r % X
    m, k = c // 2, c % 2
    pending = []

    a_copy = pltpu.make_async_copy(a_hbm, a_ref, a_sem)
    a_copy.start()

    barrier = pltpu.get_barrier_semaphore()
    for step in range(1, R):
        pl.semaphore_signal(barrier, inc=1, device_id=((r + step) % R, c), device_id_type=MESH)
    for step in range(1, C):
        pl.semaphore_signal(barrier, inc=1, device_id=(r, (c + step) % C), device_id_type=MESH)

    unit = math.gcd(rows, width)

    def mask_of(index, half):
        block = (r * rows + index * unit) // width
        node = c * (cols // width) + (half * LANES) // width
        return mask_ref[block, node].astype(jnp.float32)

    for half in range(halves):
        for index in range(rows // unit):
            there = pl.ds(index * unit, unit)
            value = factor_ref[there, half * LANES:(half + 1) * LANES].astype(jnp.float32)
            zbuf[z, half, there, :] = (value * mask_of(index, half)).astype(jnp.bfloat16)

    pl.semaphore_wait(barrier, R - 1 + C - 1)

    def start(copy, condition=None):
        pending.append((copy, condition))
        if condition is None:
            copy.start()
        else:
            pl.when(condition)(copy.start)

    def place(j):
        return j // parts, pl.ds((j % parts) * pr, pr)

    def along_z(plane, j, up, condition):
        half, span = place(j)
        piece = zbuf.at[plane, half, span]
        start(pltpu.make_async_remote_copy(
            src_ref=piece, dst_ref=piece,
            send_sem=z_send.at[0 if up else 1, plane, j], recv_sem=z_recv.at[plane, j],
            device_id=(r + X if up else r - X, c), device_id_type=MESH), condition)

    def to_owner(plane, j, condition):
        half, span = place(j)
        source = plane * X + x
        owner, g = source // G, source % G
        at = pl.multiple_of(g * rows + (j % parts) * pr, 16)
        dst = fbuf.at[half, pl.ds(at, pr), pl.ds(pl.multiple_of(c * LANES, LANES), LANES)]
        piece = zbuf.at[plane, half, span]
        here, away = owner == c, owner != c
        if condition is not None:
            here, away = jnp.logical_and(condition, here), jnp.logical_and(condition, away)
        local = pltpu.make_async_copy(piece, dst, f_recv.at[g, c, j])
        pl.when(here)(local.start)
        start(pltpu.make_async_remote_copy(
            src_ref=piece, dst_ref=dst, send_sem=b_send.at[plane, j], recv_sem=f_recv.at[g, c, j],
            device_id=(r, owner), device_id_type=MESH), away)

    def own(j):
        along_z(z, j, True, z + 1 < Z)
        along_z(z, j, False, z > 0)
        to_owner(z, j, None)

    def arrivals(j, d):
        half, span = place(j)
        for up in (True, False):
            plane = z - d if up else z + d
            there = z >= d if up else z + d < Z
            safe = jnp.clip(plane, 0, Z - 1)
            piece = zbuf.at[safe, half, span]
            pl.when(there)(pltpu.make_async_copy(piece, piece, z_recv.at[safe, j]).wait)
            if d < Z - 1:
                onward = z + 1 < Z if up else z > 0
                along_z(safe, j, up, jnp.logical_and(there, onward))
            to_owner(safe, j, there)

    def slab(g, j):
        half, _ = place(j)
        return fbuf.at[half, pl.ds(g * rows + (j % parts) * pr, pr)]

    def forward(j):
        half, _ = place(j)
        for g in range(G):
            mine = (G * c + g) % X == x
            whole = slab(g, j)

            @pl.when(mine)
            def _():
                for other in range(C):
                    piece = fbuf.at[half, pl.ds(g * rows + (j % parts) * pr, pr), pl.ds(other * LANES, LANES)]
                    pltpu.make_async_copy(piece, piece, f_recv.at[g, other, j]).wait()

            for dx in range(1, X):
                start(pltpu.make_async_remote_copy(
                    src_ref=whole, dst_ref=whole, send_sem=x_send.at[dx - 1, g, j], recv_sem=x_recv.at[g, j],
                    device_id=(z * X + (x + dx) % X, c), device_id_type=MESH), mine)

    def gather_done(half):
        for p in range(parts):
            j = half * parts + p
            for g in range(G):
                whole = slab(g, j)
                pl.when((G * c + g) % X != x)(
                    pltpu.make_async_copy(whole, whole, x_recv.at[g, j]).wait)

    def multiply(half, t):
        span = pl.ds(t * mt, mt)
        value = jnp.dot(a_ref[span, :], fbuf[half], preferred_element_type=jnp.float32)
        for other in range(C):
            part[half, other % 2, other // 2, span, :] = value[:, other * LANES:(other + 1) * LANES]
        start(pltpu.make_async_remote_copy(
            src_ref=part.at[half, 1 - k, :, span], dst_ref=pair_recv.at[half, :, span],
            send_sem=p_send.at[half, t], recv_sem=p_recv.at[half, t],
            device_id=(r, m * 2 + 1 - k), device_id_type=MESH))

    def pair_sum(half, t):
        span = pl.ds(t * mt, mt)
        piece = pair_recv.at[half, :, span]
        pltpu.make_async_copy(piece, piece, p_recv.at[half, t]).wait()
        for dm in range(1, M):
            to = (m + dm) % M
            ysend[half, dm - 1, span, :] = part[half, k, to, span, :] + pair_recv[half, to, span, :]
            start(pltpu.make_async_remote_copy(
                src_ref=ysend.at[half, dm - 1, span], dst_ref=yrecv.at[half, dm - 1, span],
                send_sem=y_send.at[half, dm - 1, t], recv_sem=y_recv.at[half, dm - 1, t],
                device_id=(r, to * 2 + k), device_id_type=MESH))

    def finish(half, t):
        span = pl.ds(t * mt, mt)
        total = part[half, k, m, span, :] + pair_recv[half, m, span, :]
        for dm in range(1, M):
            piece = yrecv.at[half, dm - 1, span]
            pltpu.make_async_copy(piece, piece, y_recv.at[half, dm - 1, t]).wait()
            total = total + yrecv[half, dm - 1, span, :]
        part[half, k, m, span, :] = total

    def correct(half):
        lanes = slice(half * LANES, (half + 1) * LANES)
        for index in range(rows // unit):
            there = pl.ds(index * unit, unit)
            value = -part[half, k, m, there, :] * mask_of(index, half)
            out_ref[there, lanes] = value.astype(jnp.bfloat16)
        for left in range(halves):
            corr[half, left * LANES:(left + 1) * LANES, :] = lax.dot_general(
                zbuf[z, left], out_ref[:, lanes], (((0,), (0,)), ((), ())),
                preferred_element_type=jnp.float32)
        for step in range(1, R):
            to = (r + step) % R
            start(pltpu.make_async_remote_copy(
                src_ref=corr.at[half, pl.ds(pl.multiple_of(to * diag_rows, 8), diag_rows)],
                dst_ref=corr_recv.at[half, step - 1],
                send_sem=c_send.at[half, step - 1], recv_sem=c_recv.at[half, step - 1],
                device_id=(to, c), device_id_type=MESH))

    def diagonal(half):
        lanes = slice(half * LANES, (half + 1) * LANES)
        total = corr[half, pl.ds(pl.multiple_of(r * diag_rows, 8), diag_rows), :]
        for step in range(1, R):
            piece = corr_recv.at[half, step - 1]
            pltpu.make_async_copy(piece, piece, c_recv.at[half, step - 1]).wait()
            total = total + corr_recv[half, step - 1]
        diag_out_ref[0, :, lanes] = diag_ref[0, :, lanes] - total

    own(0)
    jobs = []
    for j in range(J):
        for d in range(1, Z):
            arrivals(j, d)
            if d == 1 and j + 1 < J:
                own(j + 1)
        if j >= 1:
            forward(j - 1)
        for job in jobs[:3]:
            job()
        jobs = jobs[3:]
        if j >= 1 and j % parts == 0:
            half = j // parts - 1

            def ready(half=half):
                if half == 0:
                    a_copy.wait()
                gather_done(half)

            jobs.append(ready)
            for t in range(tiles):
                jobs.append(functools.partial(multiply, half, t))
            for t in range(tiles):
                jobs.append(functools.partial(pair_sum, half, t))
    forward(J - 1)
    for job in jobs:
        job()
    last = halves - 1
    for half in range(last):
        for t in range(tiles):
            finish(half, t)
        correct(half)
    if last == 0:
        a_copy.wait()
    gather_done(last)
    for t in range(tiles):
        multiply(last, t)
        if t >= 1:
            pair_sum(last, t - 1)
    pair_sum(last, tiles - 1)
    for half in range(last):
        diagonal(half)
    for t in range(tiles):
        finish(last, t)
    correct(last)
    diagonal(last)
    for copy, condition in pending:
        if condition is None:
            copy.wait_send()
        else:
            pl.when(condition)(copy.wait_send)


def body(R, C, inverse_block, factor_cols, diag_inverse, fill_mask):
    rows, cols = factor_cols.shape
    depth = inverse_block.shape[1]
    diag_rows, width = diag_inverse.shape[1:]
    X = max(n for n in range(1, R + 1) if R % n == 0 and n * n <= R)
    Z, G, M = R // X, R // C, C // 2
    halves = cols // LANES
    parts, tiles = split_rows(rows, PARTS), split_rows(rows, TILES)
    J = halves * parts
    dma = pltpu.SemaphoreType.DMA
    vmem = pl.BlockSpec(memory_space=pltpu.VMEM)
    return pl.pallas_call(
        functools.partial(kernel, R, C, X),
        out_shape=(
            jax.ShapeDtypeStruct((rows, cols), jnp.bfloat16),
            jax.ShapeDtypeStruct(diag_inverse.shape, jnp.float32),
        ),
        in_specs=[pl.BlockSpec(memory_space=pltpu.SMEM), vmem, vmem, pl.BlockSpec(memory_space=pl.ANY)],
        out_specs=(vmem, vmem),
        scratch_shapes=[
            pltpu.VMEM(inverse_block.shape, jnp.bfloat16),
            pltpu.VMEM((Z, halves, rows, LANES), jnp.bfloat16),
            pltpu.VMEM((halves, depth, C * LANES), jnp.bfloat16),
            pltpu.VMEM((halves, 2, M, rows, LANES), jnp.float32),
            pltpu.VMEM((halves, M, rows, LANES), jnp.float32),
            pltpu.VMEM((halves, max(M - 1, 1), rows, LANES), jnp.float32),
            pltpu.VMEM((halves, max(M - 1, 1), rows, LANES), jnp.float32),
            pltpu.VMEM((halves, width, LANES), jnp.float32),
            pltpu.VMEM((halves, R - 1, diag_rows, LANES), jnp.float32),
            dma(()),
            dma((2, Z, J)), dma((Z, J)), dma((Z, J)), dma((G, C, J)),
            dma((max(X - 1, 1), G, J)), dma((G, J)),
            dma((halves, tiles)), dma((halves, tiles)),
            dma((halves, max(M - 1, 1), tiles)), dma((halves, max(M - 1, 1), tiles)),
            dma((halves, R - 1)), dma((halves, R - 1)),
        ],
        compiler_params=pltpu.CompilerParams(
            collective_id=0, has_side_effects=True, vmem_limit_bytes=60 << 20
        ),
        cost_estimate=pl.CostEstimate(
            flops=2 * rows * depth * cols * C, bytes_accessed=2 * rows * depth, transcendentals=0
        ),
    )(fill_mask, factor_cols, diag_inverse, inverse_block)


def solution(mesh):
    placed = (P("row", "col"), P("row", "col"), P("col", "row", None), P())
    return jax.shard_map(
        functools.partial(body, mesh.shape["row"], mesh.shape["col"]),
        mesh=mesh,
        in_specs=placed,
        out_specs=(P("row", "col"), P("col", "row", None)),
        check_vma=False,
    )
```

time: 308 us -> 113 us (0.37)
  waiting for transfers between devices: 197 us -> 0 us
  Pallas kernels: 0 us -> 106 us
  blocking collectives: 66 us -> 0 us
  matrix products: 13.4 us -> 0 us
  between operations: 13.8 us -> 0.64 us
  other arithmetic: 5.17 us -> 0 us
  local copies, waits for them, and re-layouts: 9.69 us -> 4.71 us
    reduce_scatter x2 -> x0, waiting for transfers between devices: 109 us -> none  [the longest x1 59.5 us: body(): lax.psum_scatter(correction, 'row', scatter_dimension=1, tiled=True)]
    pallas_call x0 -> x1, Pallas kernels: none -> 106 us  [body(): pl.pallas_call(functools.partial(kernel, R, C, X), out_shape=(jax.ShapeDt...]
    all_gather x1 -> x0, waiting for transfers between devices: 87.9 us -> none  [body(): gathered_panel = lax.all_gather(selected, 'row', axis=0, tiled=True)]
    all_to_all x1 -> x0, blocking collectives: 66 us -> none  [body(): lax.all_to_all(gathered_panel, 'col', split_axis=0, concat_axis=1, tiled=...]
    dot_general x2 -> x0, matrix products: 13.4 us -> none  [the longest x1 12.3 us: body(): jnp.dot(inverse_block, spread, preferred_element_type=jnp.float32)]
    all_to_all x1 -> x0, local copies, waits for them, and re-layouts: 7.83 us -> none  [body(): lax.all_to_all(gathered_panel, 'col', split_axis=0, concat_axis=1, tiled=...]
  transfers between devices with their start and end apart: 3 -> 0, of which waited for: 3 -> 0; matrix products, arithmetic and copies ran while one was open for 0% -> 0% of each run, Pallas kernels for 0% -> 0%
where the time goes in v1:
time: 113 us; the launch traced here: 111 us
  Pallas kernels  106 us (94%)
  local copies, waits for them, and re-layouts  4.71 us (4%)
    pallas_call x1, Pallas kernels, body(): pl.pallas_call(functools.partial(kernel, R, C, X), out_shape=(jax.ShapeDt...  106 us
    unnamed x3, local copies, waits for them, and re-layouts  4.71 us

profile of v1, /device:TPU:1, one launch (start us, length us, event | category | flops | bytes accessed | tf_op | source)
XLA Modules:
  0.0 111.0 jit_solution(4708747185058761670)
XLA Ops:
  0.6 1.4 %copy.6.mask_ref = s32[40,4]{1,0:T(8,128)} copy(s32[40,4]{0,1:T(4,128)} %param.7) | data formatting | bytes 1280 | tf_op args[3]
  2.0 105.7 %shard_map.59 = (bf16[1280,256]{1,0:T(8,128)(2,1)}, f32[1,32,256]{2,1,0:T(8,128)}) custom-call(s32[40,4]{1,0:T(8,128)} %copy.6.mask_ref, bf16[1280,256]{1,0:T(8,128)(2,1)} %factor_ref.1, f32[1,32,256]{2,1,0:T(8,128)} %diag_ref.1, bf16[1280,2560]{1,0:T(8,128)(2,1)} %a_hbm.1), custom_call_target="tpu_custom_call" | custom-call | flops 6710886400 | bytes 6553600 | tf_op jit(solution)/shard_map/pallas_call | solution.py:268
  107.7 2.0 %copy.9 = bf16[1280,256]{1,0:T(8,128)(2,1)} copy(bf16[1280,256]{1,0:T(8,128)(2,1)} %get-tuple-element.4) | data formatting | bytes 1310720
  109.7 1.4 %copy.10 = f32[1,32,256]{2,1,0:T(8,128)} copy(f32[1,32,256]{2,1,0:T(8,128)} %get-tuple-element.5) | data formatting | bytes 65536

commit v2 on v1

v2 whole, which is shorter than its diff:
```python
import functools
import math

import jax
import jax.numpy as jnp
from jax import lax
from jax.experimental import pallas as pl
from jax.experimental.pallas import tpu as pltpu
from jax.sharding import PartitionSpec as P

LANES = 128
PARTS = 2
TILES = 4
DELAY = 1
MESH = pl.DeviceIdType.MESH


def split_rows(extent, most):
    return max(n for n in range(1, most + 1) if extent % n == 0 and (extent // n) % 16 == 0)


def kernel(
    R, C, X, mask_ref, factor_ref, diag_ref, a_hbm, out_ref, diag_out_ref,
    a_ref, own_ref, zbuf, fbuf, part, pair_recv, ysend, yrecv, corr, corr_recv,
    a_sem, swap_send, swap_recv, z_send, z_recv, b_send, f_recv, x_send, x_recv,
    p_send, p_recv, y_send, y_recv, c_send, c_recv,
):
    Z, G, M = R // X, R // C, C // 2
    rows, cols = factor_ref.shape
    halves = cols // LANES
    quarters = [(kk, half) for half in range(halves) for kk in range(2)]
    Q = len(quarters)
    width = diag_ref.shape[-1]
    diag_rows = diag_ref.shape[1]
    J, tiles = z_recv.shape[1], p_send.shape[1]
    parts = J // Q
    depth = rows // 2
    pr, mt = depth // parts, rows // tiles
    r, c = lax.axis_index("row"), lax.axis_index("col")
    z, x = r // X, r % X
    m, k = c // 2, c % 2
    partner = m * 2 + 1 - k
    pending = []

    a_copy = pltpu.make_async_copy(a_hbm, a_ref, a_sem)
    a_copy.start()

    barrier = pltpu.get_barrier_semaphore()
    for step in range(1, R):
        pl.semaphore_signal(barrier, inc=1, device_id=((r + step) % R, c), device_id_type=MESH)
    for step in range(1, C):
        pl.semaphore_signal(barrier, inc=1, device_id=(r, (c + step) % C), device_id_type=MESH)

    unit = math.gcd(rows, width)

    def mask_of(index, half):
        block = (r * rows + index * unit) // width
        node = c * (cols // width) + (half * LANES) // width
        return mask_ref[node, block].astype(jnp.float32)

    for half in range(halves):
        for index in range(rows // unit):
            there = pl.ds(index * unit, unit)
            value = factor_ref[there, half * LANES:(half + 1) * LANES].astype(jnp.float32)
            own_ref[half, there, :] = (value * mask_of(index, half)).astype(jnp.bfloat16)

    pl.semaphore_wait(barrier, R - 1 + C - 1)

    def start(copy, condition=None):
        pending.append((copy, condition))
        if condition is None:
            copy.start()
        else:
            pl.when(condition)(copy.start)

    def half_rows(index):
        return pl.ds(pl.multiple_of(index * depth, 16), depth)

    for half in range(halves):
        start(pltpu.make_async_remote_copy(
            src_ref=own_ref.at[half, half_rows(1 - k)], dst_ref=zbuf.at[z, half * 2 + k],
            send_sem=swap_send.at[half], recv_sem=swap_recv.at[half],
            device_id=(r, partner), device_id_type=MESH))
    for half in range(halves):
        zbuf[z, half * 2 + k] = own_ref[half, half_rows(k), :]

    def place(j):
        return j // parts, pl.ds((j % parts) * pr, pr)

    def along_z(plane, j, up, condition):
        q, span = place(j)
        piece = zbuf.at[plane, q, span]
        start(pltpu.make_async_remote_copy(
            src_ref=piece, dst_ref=piece,
            send_sem=z_send.at[0 if up else 1, plane, j], recv_sem=z_recv.at[plane, j],
            device_id=(r + X if up else r - X, c), device_id_type=MESH), condition)

    def to_owner(plane, j, condition):
        q, span = place(j)
        source = plane * X + x
        owner, g = source // G, source % G
        dst = fbuf.at[q, g, k, span, pl.ds(pl.multiple_of(m * LANES, LANES), LANES)]
        piece = zbuf.at[plane, q, span]
        here, away = owner == c, owner != c
        if condition is not None:
            here, away = jnp.logical_and(condition, here), jnp.logical_and(condition, away)
        local = pltpu.make_async_copy(piece, dst, f_recv.at[g, c, j])
        pl.when(here)(local.start)
        start(pltpu.make_async_remote_copy(
            src_ref=piece, dst_ref=dst, send_sem=b_send.at[plane, j], recv_sem=f_recv.at[g, c, j],
            device_id=(r, owner), device_id_type=MESH), away)

    def own(j):
        q = j // parts
        kk, half = quarters[q]
        if j % parts == 0:
            piece = zbuf.at[z, q]
            pl.when(k != kk)(pltpu.make_async_copy(piece, piece, swap_recv.at[half]).wait)
        along_z(z, j, True, z + 1 < Z)
        along_z(z, j, False, z > 0)
        to_owner(z, j, None)

    def arrivals(j, d):
        q, span = place(j)
        for up in (True, False):
            plane = z - d if up else z + d
            there = z >= d if up else z + d < Z
            safe = jnp.clip(plane, 0, Z - 1)
            piece = zbuf.at[safe, q, span]
            pl.when(there)(pltpu.make_async_copy(piece, piece, z_recv.at[safe, j]).wait)
            if d < Z - 1:
                onward = z + 1 < Z if up else z > 0
                along_z(safe, j, up, jnp.logical_and(there, onward))
            to_owner(safe, j, there)

    def forward(j):
        q, span = place(j)
        for g in range(G):
            mine = (G * c + g) % X == x
            whole = fbuf.at[q, g, :, span]

            @pl.when(mine)
            def _():
                for other in range(C):
                    piece = fbuf.at[q, g, other % 2, span, pl.ds(other // 2 * LANES, LANES)]
                    pltpu.make_async_copy(piece, piece, f_recv.at[g, other, j]).wait()

            for dx in range(1, X):
                start(pltpu.make_async_remote_copy(
                    src_ref=whole, dst_ref=whole, send_sem=x_send.at[dx - 1, g, j], recv_sem=x_recv.at[g, j],
                    device_id=(z * X + (x + dx) % X, c), device_id_type=MESH), mine)

    def gather_done(q):
        if q == 0:
            a_copy.wait()
        for p in range(parts):
            j = q * parts + p
            _, span = place(j)
            for g in range(G):
                whole = fbuf.at[q, g, :, span]
                pl.when((G * c + g) % X != x)(
                    pltpu.make_async_copy(whole, whole, x_recv.at[g, j]).wait)

    def multiply(q, t):
        kk, _ = quarters[q]
        span = pl.ds(t * mt, mt)
        panel = fbuf[q].reshape(G * rows, M * LANES)
        value = jnp.dot(a_ref[span, :], panel, preferred_element_type=jnp.float32)
        for to in range(M):
            part[q, to, span, :] = value[:, to * LANES:(to + 1) * LANES]
        start(pltpu.make_async_remote_copy(
            src_ref=part.at[q, :, span], dst_ref=pair_recv.at[q, :, span],
            send_sem=p_send.at[q, t], recv_sem=p_recv.at[q, t],
            device_id=(r, partner), device_id_type=MESH), k != kk)

    def pair_sum(q, t):
        kk, half = quarters[q]
        span = pl.ds(t * mt, mt)
        piece = pair_recv.at[q, :, span]

        @pl.when(k == kk)
        def _():
            pltpu.make_async_copy(piece, piece, p_recv.at[q, t]).wait()
            for dm in range(1, M):
                to = (m + dm) % M
                ysend[half, dm - 1, span, :] = part[q, to, span, :] + pair_recv[q, to, span, :]

        for dm in range(1, M):
            to = (m + dm) % M
            start(pltpu.make_async_remote_copy(
                src_ref=ysend.at[half, dm - 1, span], dst_ref=yrecv.at[half, dm - 1, span],
                send_sem=y_send.at[q, dm - 1, t], recv_sem=y_recv.at[q, dm - 1, t],
                device_id=(r, to * 2 + k), device_id_type=MESH), k == kk)

    def finish(q):
        kk, half = quarters[q]
        lanes = slice(half * LANES, (half + 1) * LANES)

        @pl.when(k == kk)
        def _():
            for t in range(tiles):
                span = pl.ds(t * mt, mt)
                total = part[q, m, span, :] + pair_recv[q, m, span, :]
                for dm in range(1, M):
                    piece = yrecv.at[half, dm - 1, span]
                    pltpu.make_async_copy(piece, piece, y_recv.at[q, dm - 1, t]).wait()
                    total = total + yrecv[half, dm - 1, span, :]
                part[q, m, span, :] = total
            for index in range(rows // unit):
                there = pl.ds(index * unit, unit)
                value = -part[q, m, there, :] * mask_of(index, half)
                out_ref[there, lanes] = value.astype(jnp.bfloat16)
            for left in range(halves):
                corr[half, left * LANES:(left + 1) * LANES, :] = lax.dot_general(
                    own_ref[left], out_ref[:, lanes], (((0,), (0,)), ((), ())),
                    preferred_element_type=jnp.float32)

        for step in range(1, R):
            to = (r + step) % R
            start(pltpu.make_async_remote_copy(
                src_ref=corr.at[half, pl.ds(pl.multiple_of(to * diag_rows, 8), diag_rows)],
                dst_ref=corr_recv.at[half, step - 1],
                send_sem=c_send.at[half, step - 1], recv_sem=c_recv.at[half, step - 1],
                device_id=(to, c), device_id_type=MESH), k == kk)

    def diagonal(q):
        kk, half = quarters[q]
        lanes = slice(half * LANES, (half + 1) * LANES)

        @pl.when(k == kk)
        def _():
            total = corr[half, pl.ds(pl.multiple_of(r * diag_rows, 8), diag_rows), :]
            for step in range(1, R):
                piece = corr_recv.at[half, step - 1]
                pltpu.make_async_copy(piece, piece, c_recv.at[half, step - 1]).wait()
                total = total + corr_recv[half, step - 1]
            diag_out_ref[0, :, lanes] = diag_ref[0, :, lanes] - total

    def work(q):
        def first():
            gather_done(q)
            multiply(q, 0)

        def sums():
            for t in range(tiles):
                pair_sum(q, t)

        jobs = [first] + [functools.partial(multiply, q, t) for t in range(1, tiles)] + [sums]
        if q >= 1:
            jobs.append(functools.partial(finish, q - 1))
        return jobs

    own(0)
    jobs, done = [], 0
    for j in range(J):
        for d in range(1, Z):
            arrivals(j, d)
            if d == 1 and j + 1 < J:
                own(j + 1)
            if jobs:
                jobs.pop(0)()
        if j >= 1:
            forward(j - 1)
        if j - DELAY >= (done + 1) * parts:
            jobs += work(done)
            done += 1
    forward(J - 1)
    for job in jobs:
        job()
    for q in range(done, Q):
        gather_done(q)
        for t in range(tiles):
            multiply(q, t)
            if t >= 1:
                pair_sum(q, t - 1)
        pair_sum(q, tiles - 1)
        if q >= 1:
            finish(q - 1)
    for q in range(Q - 1):
        diagonal(q)
    finish(Q - 1)
    diagonal(Q - 1)
    for copy, condition in pending:
        if condition is None:
            copy.wait_send()
        else:
            pl.when(condition)(copy.wait_send)


def body(R, C, inverse_block, factor_cols, diag_inverse, fill_mask):
    rows, cols = factor_cols.shape
    depth = inverse_block.shape[1]
    diag_rows, width = diag_inverse.shape[1:]
    X = max(n for n in range(1, R + 1) if R % n == 0 and n * n <= R)
    Z, G, M = R // X, R // C, C // 2
    halves = cols // LANES
    parts, tiles = split_rows(rows // 2, PARTS), split_rows(rows, TILES)
    Q = 2 * halves
    J = Q * parts
    dma = pltpu.SemaphoreType.DMA
    vmem = pl.BlockSpec(memory_space=pltpu.VMEM)
    return pl.pallas_call(
        functools.partial(kernel, R, C, X),
        out_shape=(
            jax.ShapeDtypeStruct((rows, cols), jnp.bfloat16),
            jax.ShapeDtypeStruct(diag_inverse.shape, jnp.float32),
        ),
        in_specs=[pl.BlockSpec(memory_space=pltpu.SMEM), vmem, vmem, pl.BlockSpec(memory_space=pl.ANY)],
        out_specs=(vmem, vmem),
        scratch_shapes=[
            pltpu.VMEM(inverse_block.shape, jnp.bfloat16),
            pltpu.VMEM((halves, rows, LANES), jnp.bfloat16),
            pltpu.VMEM((Z, Q, rows // 2, LANES), jnp.bfloat16),
            pltpu.VMEM((Q, G, 2, rows // 2, M * LANES), jnp.bfloat16),
            pltpu.VMEM((Q, M, rows, LANES), jnp.float32),
            pltpu.VMEM((Q, M, rows, LANES), jnp.float32),
            pltpu.VMEM((halves, max(M - 1, 1), rows, LANES), jnp.float32),
            pltpu.VMEM((halves, max(M - 1, 1), rows, LANES), jnp.float32),
            pltpu.VMEM((halves, width, LANES), jnp.float32),
            pltpu.VMEM((halves, R - 1, diag_rows, LANES), jnp.float32),
            dma(()), dma((halves,)), dma((halves,)),
            dma((2, Z, J)), dma((Z, J)), dma((Z, J)), dma((G, C, J)),
            dma((max(X - 1, 1), G, J)), dma((G, J)),
            dma((Q, tiles)), dma((Q, tiles)),
            dma((Q, max(M - 1, 1), tiles)), dma((Q, max(M - 1, 1), tiles)),
            dma((halves, R - 1)), dma((halves, R - 1)),
        ],
        compiler_params=pltpu.CompilerParams(
            collective_id=0, has_side_effects=True, vmem_limit_bytes=60 << 20
        ),
        cost_estimate=pl.CostEstimate(
            flops=2 * rows * depth * cols * C, bytes_accessed=2 * rows * depth, transcendentals=0
        ),
    )(fill_mask.T, factor_cols, diag_inverse, inverse_block)


def solution(mesh):
    placed = (P("row", "col"), P("row", "col"), P("col", "row", None), P())
    return jax.shard_map(
        functools.partial(body, mesh.shape["row"], mesh.shape["col"]),
        mesh=mesh,
        in_specs=placed,
        out_specs=(P("row", "col"), P("col", "row", None)),
        check_vma=False,
    )
```

time: 113 us -> 106 us (0.938); the launches traced: 111 us -> 105 us
  Pallas kernels: 106 us -> 102 us
  local copies, waits for them, and re-layouts: 4.71 us -> 3.34 us
    pallas_call x1, Pallas kernels: 106 us -> 102 us  [body(): pl.pallas_call(functools.partial(kernel, R, C, X), out_shape=(jax.ShapeDt...]
    unnamed x3 -> x2, local copies, waits for them, and re-layouts: 4.71 us -> 3.34 us
where the time goes in v2:
time: 106 us; the launch traced here: 105 us
  Pallas kernels  102 us (96%)
  local copies, waits for them, and re-layouts  3.34 us (3%)
    pallas_call x1, Pallas kernels, body(): pl.pallas_call(functools.partial(kernel, R, C, X), out_shape=(jax.ShapeDt...  102 us
    unnamed x2, local copies, waits for them, and re-layouts  3.34 us

profile of v2, /device:TPU:1, one launch (start us, length us, event | category | flops | bytes accessed | tf_op | source)
XLA Modules:
  0.0 105.5 jit_solution(9090094762771688997)
XLA Ops:
  0.6 101.5 %shard_map.59 = (bf16[1280,256]{1,0:T(8,128)(2,1)}, f32[1,32,256]{2,1,0:T(8,128)}) custom-call(s32[4,40]{1,0:T(4,128)} %bitcast.1, bf16[1280,256]{1,0:T(8,128)(2,1)} %factor_ref.1, f32[1,32,256]{2,1,0:T(8,128)} %diag_ref.1, bf16[1280,2560]{1,0:T(8,128)(2,1)} %a_hbm.1), custom_call_target="tpu_custom_call" | custom-call | flops 6710886400 | bytes 6553600 | tf_op jit(solution)/shard_map/pallas_call | solution.py:302
  102.2 2.0 %copy.8 = bf16[1280,256]{1,0:T(8,128)(2,1)} copy(bf16[1280,256]{1,0:T(8,128)(2,1)} %get-tuple-element.4) | data formatting | bytes 1310720
  104.1 1.4 %copy.9 = f32[1,32,256]{2,1,0:T(8,128)} copy(f32[1,32,256]{2,1,0:T(8,128)} %get-tuple-element.5) | data formatting | bytes 65536

commit v3 on v2

--- a/solution.py
+++ b/solution.py
@@ -12,6 +12,8 @@
 PARTS = 2
 TILES = 4
 DELAY = 1
+HOPS = 2
+AHEAD = 2
 MESH = pl.DeviceIdType.MESH
 
 
@@ -87,13 +89,13 @@
     def place(j):
         return j // parts, pl.ds((j % parts) * pr, pr)
 
-    def along_z(plane, j, up, condition):
+    def along_z(plane, j, up, hops, condition):
         q, span = place(j)
         piece = zbuf.at[plane, q, span]
         start(pltpu.make_async_remote_copy(
             src_ref=piece, dst_ref=piece,
-            send_sem=z_send.at[0 if up else 1, plane, j], recv_sem=z_recv.at[plane, j],
-            device_id=(r + X if up else r - X, c), device_id_type=MESH), condition)
+            send_sem=z_send.at[hops - 1, 0 if up else 1, plane, j], recv_sem=z_recv.at[plane, j],
+            device_id=(r + X * hops if up else r - X * hops, c), device_id_type=MESH), condition)
 
     def to_owner(plane, j, condition):
         q, span = place(j)
@@ -116,8 +118,9 @@
         if j % parts == 0:
             piece = zbuf.at[z, q]
             pl.when(k != kk)(pltpu.make_async_copy(piece, piece, swap_recv.at[half]).wait)
-        along_z(z, j, True, z + 1 < Z)
-        along_z(z, j, False, z > 0)
+        for hops in range(1, HOPS + 1):
+            along_z(z, j, True, hops, z + hops < Z)
+            along_z(z, j, False, hops, z >= hops)
         to_owner(z, j, None)
 
     def arrivals(j, d):
@@ -128,9 +131,9 @@
             safe = jnp.clip(plane, 0, Z - 1)
             piece = zbuf.at[safe, q, span]
             pl.when(there)(pltpu.make_async_copy(piece, piece, z_recv.at[safe, j]).wait)
-            if d < Z - 1:
+            if HOPS <= d < Z - 1:
                 onward = z + 1 < Z if up else z > 0
-                along_z(safe, j, up, jnp.logical_and(there, onward))
+                along_z(safe, j, up, 1, jnp.logical_and(there, onward))
             to_owner(safe, j, there)
 
     def forward(j):
@@ -250,13 +253,14 @@
             jobs.append(functools.partial(finish, q - 1))
         return jobs
 
-    own(0)
+    for j in range(min(AHEAD, J)):
+        own(j)
     jobs, done = [], 0
     for j in range(J):
         for d in range(1, Z):
             arrivals(j, d)
-            if d == 1 and j + 1 < J:
-                own(j + 1)
+            if d == 1 and j + AHEAD < J:
+                own(j + AHEAD)
             if jobs:
                 jobs.pop(0)()
         if j >= 1:
@@ -319,7 +323,7 @@
             pltpu.VMEM((halves, width, LANES), jnp.float32),
             pltpu.VMEM((halves, R - 1, diag_rows, LANES), jnp.float32),
             dma(()), dma((halves,)), dma((halves,)),
-            dma((2, Z, J)), dma((Z, J)), dma((Z, J)), dma((G, C, J)),
+            dma((HOPS, 2, Z, J)), dma((Z, J)), dma((Z, J)), dma((G, C, J)),
             dma((max(X - 1, 1), G, J)), dma((G, J)),
             dma((Q, tiles)), dma((Q, tiles)),
             dma((Q, max(M - 1, 1), tiles)), dma((Q, max(M - 1, 1), tiles)),

time: 106 us -> 108 us (1.019)
    pallas_call x1, Pallas kernels: 102 us -> 103 us  [body(): pl.pallas_call(functools.partial(kernel, R, C, X), out_shape=(jax.ShapeDt...]
where the time goes in v3:
time: 108 us; the launch traced here: 107 us
  Pallas kernels  103 us (95%)
  local copies, waits for them, and re-layouts  3.34 us (3%)
    pallas_call x1, Pallas kernels, body(): pl.pallas_call(functools.partial(kernel, R, C, X), out_shape=(jax.ShapeDt...  103 us
    unnamed x2, local copies, waits for them, and re-layouts  3.34 us

profile of v3, /device:TPU:1, one launch (start us, length us, event | category | flops | bytes accessed | tf_op | source)
XLA Modules:
  0.0 107.3 jit_solution(9949574795177348710)
XLA Ops:
  0.6 103.3 %shard_map.59 = (bf16[1280,256]{1,0:T(8,128)(2,1)}, f32[1,32,256]{2,1,0:T(8,128)}) custom-call(s32[4,40]{1,0:T(4,128)} %bitcast.1, bf16[1280,256]{1,0:T(8,128)(2,1)} %factor_ref.1, f32[1,32,256]{2,1,0:T(8,128)} %diag_ref.1, bf16[1280,2560]{1,0:T(8,128)(2,1)} %a_hbm.1), custom_call_target="tpu_custom_call" | custom-call | flops 6710886400 | bytes 6553600 | tf_op jit(solution)/shard_map/pallas_call | solution.py:306
  104.0 2.0 %copy.8 = bf16[1280,256]{1,0:T(8,128)(2,1)} copy(bf16[1280,256]{1,0:T(8,128)(2,1)} %get-tuple-element.4) | data formatting | bytes 1310720
  105.9 1.4 %copy.9 = f32[1,32,256]{2,1,0:T(8,128)} copy(f32[1,32,256]{2,1,0:T(8,128)} %get-tuple-element.5) | data formatting | bytes 65536

commit v4 on v3

--- a/solution.py
+++ b/solution.py
@@ -11,9 +11,11 @@
 LANES = 128
 PARTS = 2
 TILES = 4
+COPIES = 4
 DELAY = 1
-HOPS = 2
-AHEAD = 2
+HOPS = 1
+AHEAD = 1
+EARLY = 2
 MESH = pl.DeviceIdType.MESH
 
 
@@ -24,7 +26,7 @@
 def kernel(
     R, C, X, mask_ref, factor_ref, diag_ref, a_hbm, out_ref, diag_out_ref,
     a_ref, own_ref, zbuf, fbuf, part, pair_recv, ysend, yrecv, corr, corr_recv,
-    a_sem, swap_send, swap_recv, z_send, z_recv, b_send, f_recv, x_send, x_recv,
+    a_sem, swap_send, swap_recv, e_send, e_recv, z_send, z_recv, b_send, f_recv, x_send, x_recv,
     p_send, p_recv, y_send, y_recv, c_send, c_recv,
 ):
     Z, G, M = R // X, R // C, C // 2
@@ -34,7 +36,7 @@
     Q = len(quarters)
     width = diag_ref.shape[-1]
     diag_rows = diag_ref.shape[1]
-    J, tiles = z_recv.shape[1], p_send.shape[1]
+    J, tiles = z_recv.shape[2], p_send.shape[1]
     parts = J // Q
     depth = rows // 2
     pr, mt = depth // parts, rows // tiles
@@ -80,74 +82,101 @@
 
     for half in range(halves):
         start(pltpu.make_async_remote_copy(
-            src_ref=own_ref.at[half, half_rows(1 - k)], dst_ref=zbuf.at[z, half * 2 + k],
+            src_ref=own_ref.at[half, half_rows(1 - k)], dst_ref=zbuf.at[z, x, half * 2 + k],
             send_sem=swap_send.at[half], recv_sem=swap_recv.at[half],
             device_id=(r, partner), device_id_type=MESH))
     for half in range(halves):
-        zbuf[z, half * 2 + k] = own_ref[half, half_rows(k), :]
+        zbuf[z, x, half * 2 + k] = own_ref[half, half_rows(k), :]
 
     def place(j):
         return j // parts, pl.ds((j % parts) * pr, pr)
 
-    def along_z(plane, j, up, hops, condition):
-        q, span = place(j)
-        piece = zbuf.at[plane, q, span]
+    def early(j):
+        return j >= J - EARLY
+
+    def sources(j):
+        return [x] + [(x + dx) % X for dx in range(1, X) if early(j)]
+
+    def along_z(plane, xs, j, up, hops, condition):
+        q, span = place(j)
+        piece = zbuf.at[plane, xs, q, span]
         start(pltpu.make_async_remote_copy(
             src_ref=piece, dst_ref=piece,
-            send_sem=z_send.at[hops - 1, 0 if up else 1, plane, j], recv_sem=z_recv.at[plane, j],
+            send_sem=z_send.at[hops - 1, 0 if up else 1, plane, xs, j], recv_sem=z_recv.at[plane, xs, j],
             device_id=(r + X * hops if up else r - X * hops, c), device_id_type=MESH), condition)
 
-    def to_owner(plane, j, condition):
-        q, span = place(j)
-        source = plane * X + x
+    def to_owner(plane, xs, j, condition):
+        q, span = place(j)
+        source = plane * X + xs
         owner, g = source // G, source % G
         dst = fbuf.at[q, g, k, span, pl.ds(pl.multiple_of(m * LANES, LANES), LANES)]
-        piece = zbuf.at[plane, q, span]
+        piece = zbuf.at[plane, xs, q, span]
         here, away = owner == c, owner != c
         if condition is not None:
             here, away = jnp.logical_and(condition, here), jnp.logical_and(condition, away)
         local = pltpu.make_async_copy(piece, dst, f_recv.at[g, c, j])
         pl.when(here)(local.start)
         start(pltpu.make_async_remote_copy(
-            src_ref=piece, dst_ref=dst, send_sem=b_send.at[plane, j], recv_sem=f_recv.at[g, c, j],
+            src_ref=piece, dst_ref=dst, send_sem=b_send.at[plane, xs, j], recv_sem=f_recv.at[g, c, j],
             device_id=(r, owner), device_id_type=MESH), away)
 
+    def swapped(q):
+        kk, half = quarters[q]
+        piece = zbuf.at[z, x, q]
+        pl.when(k != kk)(pltpu.make_async_copy(piece, piece, swap_recv.at[half]).wait)
+
+    def across(j):
+        q, span = place(j)
+        for dx in range(1, X):
+            piece = zbuf.at[z, x, q, span]
+            start(pltpu.make_async_remote_copy(
+                src_ref=piece, dst_ref=piece,
+                send_sem=e_send.at[dx - 1, j - (J - EARLY)], recv_sem=e_recv.at[x, j - (J - EARLY)],
+                device_id=(z * X + (x + dx) % X, c), device_id_type=MESH))
+
     def own(j):
-        q = j // parts
-        kk, half = quarters[q]
-        if j % parts == 0:
-            piece = zbuf.at[z, q]
-            pl.when(k != kk)(pltpu.make_async_copy(piece, piece, swap_recv.at[half]).wait)
-        for hops in range(1, HOPS + 1):
-            along_z(z, j, True, hops, z + hops < Z)
-            along_z(z, j, False, hops, z >= hops)
-        to_owner(z, j, None)
+        q, span = place(j)
+        if j % parts == 0 and q not in swaps:
+            swapped(q)
+            swaps.add(q)
+        for xs in sources(j):
+            if xs is not x:
+                piece = zbuf.at[z, xs, q, span]
+                pltpu.make_async_copy(piece, piece, e_recv.at[xs, j - (J - EARLY)]).wait()
+            for hops in range(1, HOPS + 1):
+                along_z(z, xs, j, True, hops, z + hops < Z)
+                along_z(z, xs, j, False, hops, z >= hops)
+            to_owner(z, xs, j, None)
 
     def arrivals(j, d):
         q, span = place(j)
-        for up in (True, False):
-            plane = z - d if up else z + d
-            there = z >= d if up else z + d < Z
-            safe = jnp.clip(plane, 0, Z - 1)
-            piece = zbuf.at[safe, q, span]
-            pl.when(there)(pltpu.make_async_copy(piece, piece, z_recv.at[safe, j]).wait)
-            if HOPS <= d < Z - 1:
-                onward = z + 1 < Z if up else z > 0
-                along_z(safe, j, up, 1, jnp.logical_and(there, onward))
-            to_owner(safe, j, there)
+        for xs in sources(j):
+            for up in (True, False):
+                plane = z - d if up else z + d
+                there = z >= d if up else z + d < Z
+                safe = jnp.clip(plane, 0, Z - 1)
+                piece = zbuf.at[safe, xs, q, span]
+                pl.when(there)(pltpu.make_async_copy(piece, piece, z_recv.at[safe, xs, j]).wait)
+                if HOPS <= d < Z - 1:
+                    onward = z + 1 < Z if up else z > 0
+                    along_z(safe, xs, j, up, 1, jnp.logical_and(there, onward))
+                to_owner(safe, xs, j, there)
+
+    def collected(g, j):
+        q, span = place(j)
+        for other in range(C):
+            piece = fbuf.at[q, g, other % 2, span, pl.ds(other // 2 * LANES, LANES)]
+            pltpu.make_async_copy(piece, piece, f_recv.at[g, other, j]).wait()
 
     def forward(j):
+        if early(j):
+            return
         q, span = place(j)
         for g in range(G):
             mine = (G * c + g) % X == x
             whole = fbuf.at[q, g, :, span]
 
-            @pl.when(mine)
-            def _():
-                for other in range(C):
-                    piece = fbuf.at[q, g, other % 2, span, pl.ds(other // 2 * LANES, LANES)]
-                    pltpu.make_async_copy(piece, piece, f_recv.at[g, other, j]).wait()
-
+            pl.when(mine)(functools.partial(collected, g, j))
             for dx in range(1, X):
                 start(pltpu.make_async_remote_copy(
                     src_ref=whole, dst_ref=whole, send_sem=x_send.at[dx - 1, g, j], recv_sem=x_recv.at[g, j],
@@ -160,6 +189,9 @@
             j = q * parts + p
             _, span = place(j)
             for g in range(G):
+                if early(j):
+                    collected(g, j)
+                    continue
                 whole = fbuf.at[q, g, :, span]
                 pl.when((G * c + g) % X != x)(
                     pltpu.make_async_copy(whole, whole, x_recv.at[g, j]).wait)
@@ -253,8 +285,14 @@
             jobs.append(functools.partial(finish, q - 1))
         return jobs
 
+    swaps = set()
     for j in range(min(AHEAD, J)):
         own(j)
+    for j in range(J - EARLY, J):
+        if j // parts not in swaps:
+            swapped(j // parts)
+            swaps.add(j // parts)
+        across(j)
     jobs, done = [], 0
     for j in range(J):
         for d in range(1, Z):
@@ -291,6 +329,18 @@
             pl.when(condition)(copy.wait_send)
 
 
+def hand_over(cols_ref, diag_ref, cols_out, diag_out, sems):
+    rows = cols_ref.shape[0] // COPIES
+    copies = [pltpu.make_async_copy(diag_ref, diag_out, sems.at[COPIES])]
+    for n in range(COPIES):
+        span = pl.ds(n * rows, rows)
+        copies.append(pltpu.make_async_copy(cols_ref.at[span], cols_out.at[span], sems.at[n]))
+    for copy in copies:
+        copy.start()
+    for copy in copies:
+        copy.wait()
+
+
 def body(R, C, inverse_block, factor_cols, diag_inverse, fill_mask):
     rows, cols = factor_cols.shape
     depth = inverse_block.shape[1]
@@ -303,18 +353,19 @@
     J = Q * parts
     dma = pltpu.SemaphoreType.DMA
     vmem = pl.BlockSpec(memory_space=pltpu.VMEM)
-    return pl.pallas_call(
+    out_shape = (
+        jax.ShapeDtypeStruct((rows, cols), jnp.bfloat16),
+        jax.ShapeDtypeStruct(diag_inverse.shape, jnp.float32),
+    )
+    results = pl.pallas_call(
         functools.partial(kernel, R, C, X),
-        out_shape=(
-            jax.ShapeDtypeStruct((rows, cols), jnp.bfloat16),
-            jax.ShapeDtypeStruct(diag_inverse.shape, jnp.float32),
-        ),
+        out_shape=out_shape,
         in_specs=[pl.BlockSpec(memory_space=pltpu.SMEM), vmem, vmem, pl.BlockSpec(memory_space=pl.ANY)],
         out_specs=(vmem, vmem),
         scratch_shapes=[
             pltpu.VMEM(inverse_block.shape, jnp.bfloat16),
             pltpu.VMEM((halves, rows, LANES), jnp.bfloat16),
-            pltpu.VMEM((Z, Q, rows // 2, LANES), jnp.bfloat16),
+            pltpu.VMEM((Z, X, Q, rows // 2, LANES), jnp.bfloat16),
             pltpu.VMEM((Q, G, 2, rows // 2, M * LANES), jnp.bfloat16),
             pltpu.VMEM((Q, M, rows, LANES), jnp.float32),
             pltpu.VMEM((Q, M, rows, LANES), jnp.float32),
@@ -323,7 +374,8 @@
             pltpu.VMEM((halves, width, LANES), jnp.float32),
             pltpu.VMEM((halves, R - 1, diag_rows, LANES), jnp.float32),
             dma(()), dma((halves,)), dma((halves,)),
-            dma((HOPS, 2, Z, J)), dma((Z, J)), dma((Z, J)), dma((G, C, J)),
+            dma((max(X - 1, 1), EARLY)), dma((X, EARLY)),
+            dma((HOPS, 2, Z, X, J)), dma((Z, X, J)), dma((Z, X, J)), dma((G, C, J)),
             dma((max(X - 1, 1), G, J)), dma((G, J)),
             dma((Q, tiles)), dma((Q, tiles)),
             dma((Q, max(M - 1, 1), tiles)), dma((Q, max(M - 1, 1), tiles)),
@@ -336,6 +388,14 @@
             flops=2 * rows * depth * cols * C, bytes_accessed=2 * rows * depth, transcendentals=0
         ),
     )(fill_mask.T, factor_cols, diag_inverse, inverse_block)
+    anywhere = pl.BlockSpec(memory_space=pl.ANY)
+    return pl.pallas_call(
+        hand_over,
+        out_shape=out_shape,
+        in_specs=[anywhere, anywhere],
+        out_specs=(anywhere, anywhere),
+        scratch_shapes=[dma((COPIES + 1,))],
+    )(*results)
 
 
 def solution(mesh):

time: 108 us -> 124 us (1.15)
  Pallas kernels: 103 us -> 123 us
  local copies, waits for them, and re-layouts: 3.34 us -> 0 us
    pallas_call x1 -> x2, Pallas kernels: 103 us -> 123 us  [the longest x1 101 us: body(): pl.pallas_call(functools.partial(kernel, R, C, X), out_shape=out_shape, i...]
    unnamed x2 -> x0, local copies, waits for them, and re-layouts: 3.34 us -> none
where the time goes in v4:
time: 124 us
  Pallas kernels  123 us (99%)
    pallas_call x1, Pallas kernels, body(): pl.pallas_call(functools.partial(kernel, R, C, X), out_shape=out_shape, i...  101 us
    pallas_call x1, Pallas kernels, body(): pl.pallas_call(hand_over, out_shape=out_shape, in_specs=[anywhere, anywhe...  22 us

profile of v4, /device:TPU:1, one launch (start us, length us, event | category | flops | bytes accessed | tf_op | source)
XLA Modules:
  0.0 123.6 jit_solution(4159906892476018238)
XLA Ops:
  0.6 100.8 %shard_map.59 = (bf16[1280,256]{1,0:T(8,128)(2,1)}, f32[1,32,256]{2,1,0:T(8,128)}) custom-call(s32[4,40]{1,0:T(4,128)} %bitcast.1, bf16[1280,256]{1,0:T(8,128)(2,1)} %factor_ref.1, f32[1,32,256]{2,1,0:T(8,128)} %diag_ref.1, bf16[1280,2560]{1,0:T(8,128)(2,1)} %a_hbm.1), custom_call_target="tpu_custom_call" | custom-call | flops 6710886400 | bytes 6553600 | tf_op jit(solution)/shard_map/pallas_call | solution.py:360
  101.5 22.0 %shard_map.60 = (bf16[1280,256]{1,0:T(8,128)(2,1)}, f32[1,32,256]{2,1,0:T(8,128)}) custom-call(bf16[1280,256]{1,0:T(8,128)(2,1)} %get-tuple-element.4.cols_ref, f32[1,32,256]{2,1,0:T(8,128)} %get-tuple-element.5.diag_ref), custom_call_target="tpu_custom_call" | custom-call | tf_op jit(solution)/shard_map/pallas_call | solution.py:392

commit v5 on v4

--- a/solution.py
+++ b/solution.py
@@ -10,12 +10,11 @@
 
 LANES = 128
 PARTS = 2
-TILES = 4
-COPIES = 4
+TILES = 5
 DELAY = 1
 HOPS = 1
 AHEAD = 1
-EARLY = 2
+EARLY = 1
 MESH = pl.DeviceIdType.MESH
 
 
@@ -182,7 +181,7 @@
                     src_ref=whole, dst_ref=whole, send_sem=x_send.at[dx - 1, g, j], recv_sem=x_recv.at[g, j],
                     device_id=(z * X + (x + dx) % X, c), device_id_type=MESH), mine)
 
-    def gather_done(q):
+    def gather_done(q, begun=False):
         if q == 0:
             a_copy.wait()
         for p in range(parts):
@@ -190,23 +189,56 @@
             _, span = place(j)
             for g in range(G):
                 if early(j):
-                    collected(g, j)
+                    if begun:
+                        pl.when(jnp.logical_not(mine(g)))(functools.partial(collected, g, j))
+                    else:
+                        collected(g, j)
                     continue
                 whole = fbuf.at[q, g, :, span]
                 pl.when((G * c + g) % X != x)(
                     pltpu.make_async_copy(whole, whole, x_recv.at[g, j]).wait)
 
+    def mine(g):
+        return (G * c + g) % X == x
+
+    def add_group(q, g, t):
+        span = pl.ds(t * mt, mt)
+        panel = fbuf[q, g].reshape(rows, M * LANES)
+        value = jnp.dot(a_ref[span, g * rows:(g + 1) * rows], panel, preferred_element_type=jnp.float32)
+        for to in range(M):
+            part[q, to, span, :] += value[:, to * LANES:(to + 1) * LANES]
+
+    def begin(q):
+        part[q] = jnp.zeros(part.shape[1:], jnp.float32)
+        for g in range(G):
+            @pl.when(mine(g))
+            def _():
+                for p in range(parts):
+                    if early(q * parts + p):
+                        collected(g, q * parts + p)
+                for t in range(tiles):
+                    add_group(q, g, t)
+
+    def complete(q, t):
+        for g in range(G):
+            pl.when(jnp.logical_not(mine(g)))(functools.partial(add_group, q, g, t))
+        send_pair(q, t)
+
+    def send_pair(q, t):
+        kk, _ = quarters[q]
+        span = pl.ds(t * mt, mt)
+        start(pltpu.make_async_remote_copy(
+            src_ref=part.at[q, :, span], dst_ref=pair_recv.at[q, :, span],
+            send_sem=p_send.at[q, t], recv_sem=p_recv.at[q, t],
+            device_id=(r, partner), device_id_type=MESH), k != kk)
+
     def multiply(q, t):
-        kk, _ = quarters[q]
         span = pl.ds(t * mt, mt)
         panel = fbuf[q].reshape(G * rows, M * LANES)
         value = jnp.dot(a_ref[span, :], panel, preferred_element_type=jnp.float32)
         for to in range(M):
             part[q, to, span, :] = value[:, to * LANES:(to + 1) * LANES]
-        start(pltpu.make_async_remote_copy(
-            src_ref=part.at[q, :, span], dst_ref=pair_recv.at[q, :, span],
-            send_sem=p_send.at[q, t], recv_sem=p_recv.at[q, t],
-            device_id=(r, partner), device_id_type=MESH), k != kk)
+        send_pair(q, t)
 
     def pair_sum(q, t):
         kk, half = quarters[q]
@@ -240,15 +272,18 @@
                     piece = yrecv.at[half, dm - 1, span]
                     pltpu.make_async_copy(piece, piece, y_recv.at[q, dm - 1, t]).wait()
                     total = total + yrecv[half, dm - 1, span, :]
-                part[q, m, span, :] = total
-            for index in range(rows // unit):
-                there = pl.ds(index * unit, unit)
-                value = -part[q, m, there, :] * mask_of(index, half)
-                out_ref[there, lanes] = value.astype(jnp.bfloat16)
-            for left in range(halves):
-                corr[half, left * LANES:(left + 1) * LANES, :] = lax.dot_general(
-                    own_ref[left], out_ref[:, lanes], (((0,), (0,)), ((), ())),
-                    preferred_element_type=jnp.float32)
+                for index in range(mt // unit):
+                    value = -total[index * unit:(index + 1) * unit] * mask_of(t * (mt // unit) + index, half)
+                    out_ref[pl.ds(t * mt + index * unit, unit), lanes] = value.astype(jnp.bfloat16)
+                for left in range(halves):
+                    there = slice(left * LANES, (left + 1) * LANES)
+                    product = lax.dot_general(
+                        own_ref[left, span, :], out_ref[span, lanes], (((0,), (0,)), ((), ())),
+                        preferred_element_type=jnp.float32)
+                    if t == 0:
+                        corr[half, there, :] = product
+                    else:
+                        corr[half, there, :] += product
 
         for step in range(1, R):
             to = (r + step) % R
@@ -299,10 +334,10 @@
             arrivals(j, d)
             if d == 1 and j + AHEAD < J:
                 own(j + AHEAD)
+            if d == max(Z - 2, 1) and j >= 1:
+                forward(j - 1)
             if jobs:
                 jobs.pop(0)()
-        if j >= 1:
-            forward(j - 1)
         if j - DELAY >= (done + 1) * parts:
             jobs += work(done)
             done += 1
@@ -310,9 +345,12 @@
     for job in jobs:
         job()
     for q in range(done, Q):
-        gather_done(q)
+        last = q == Q - 1 and q > 0
+        if last:
+            begin(q)
+        gather_done(q, last)
         for t in range(tiles):
-            multiply(q, t)
+            (complete if last else multiply)(q, t)
             if t >= 1:
                 pair_sum(q, t - 1)
         pair_sum(q, tiles - 1)
@@ -329,16 +367,9 @@
             pl.when(condition)(copy.wait_send)
 
 
-def hand_over(cols_ref, diag_ref, cols_out, diag_out, sems):
-    rows = cols_ref.shape[0] // COPIES
-    copies = [pltpu.make_async_copy(diag_ref, diag_out, sems.at[COPIES])]
-    for n in range(COPIES):
-        span = pl.ds(n * rows, rows)
-        copies.append(pltpu.make_async_copy(cols_ref.at[span], cols_out.at[span], sems.at[n]))
-    for copy in copies:
-        copy.start()
-    for copy in copies:
-        copy.wait()
+def hand_over(cols_ref, diag_ref, cols_out, diag_out):
+    cols_out[...] = cols_ref[...]
+    diag_out[...] = diag_ref[...]
 
 
 def body(R, C, inverse_block, factor_cols, diag_inverse, fill_mask):
@@ -348,7 +379,9 @@
     X = max(n for n in range(1, R + 1) if R % n == 0 and n * n <= R)
     Z, G, M = R // X, R // C, C // 2
     halves = cols // LANES
-    parts, tiles = split_rows(rows // 2, PARTS), split_rows(rows, TILES)
+    parts = split_rows(rows // 2, PARTS)
+    blocks = rows // math.gcd(rows, width)
+    tiles = max(n for n in range(1, TILES + 1) if blocks % n == 0)
     Q = 2 * halves
     J = Q * parts
     dma = pltpu.SemaphoreType.DMA
@@ -388,13 +421,11 @@
             flops=2 * rows * depth * cols * C, bytes_accessed=2 * rows * depth, transcendentals=0
         ),
     )(fill_mask.T, factor_cols, diag_inverse, inverse_block)
-    anywhere = pl.BlockSpec(memory_space=pl.ANY)
     return pl.pallas_call(
         hand_over,
         out_shape=out_shape,
-        in_specs=[anywhere, anywhere],
-        out_specs=(anywhere, anywhere),
-        scratch_shapes=[dma((COPIES + 1,))],
+        in_specs=[vmem, vmem],
+        out_specs=(vmem, vmem),
     )(*results)
 
 

time: 124 us -> 101 us (0.81)
  Pallas kernels: 123 us -> 100 us
    pallas_call x1, Pallas kernels: 22 us -> 1.97 us  [body(): pl.pallas_call(hand_over, out_shape=out_shape, in_specs=[vmem, vmem], out...]
    pallas_call x1, Pallas kernels: 101 us -> 98.5 us  [body(): pl.pallas_call(functools.partial(kernel, R, C, X), out_shape=out_shape, i...]
where the time goes in v5:
time: 101 us
  Pallas kernels  100 us (99%)
    pallas_call x1, Pallas kernels, body(): pl.pallas_call(functools.partial(kernel, R, C, X), out_shape=out_shape, i...  98.5 us

profile of v5, /device:TPU:1, one launch (start us, length us, event | category | flops | bytes accessed | tf_op | source)
XLA Modules:
  0.0 101.1 jit_solution(17809540140547679715)
XLA Ops:
  0.6 98.5 %shard_map.59 = (bf16[1280,256]{1,0:T(8,128)(2,1)}, f32[1,32,256]{2,1,0:T(8,128)}) custom-call(s32[4,40]{1,0:T(4,128)} %bitcast.1, bf16[1280,256]{1,0:T(8,128)(2,1)} %factor_ref.1, f32[1,32,256]{2,1,0:T(8,128)} %diag_ref.1, bf16[1280,2560]{1,0:T(8,128)(2,1)} %a_hbm.1), custom_call_target="tpu_custom_call" | custom-call | flops 6710886400 | bytes 6553600 | tf_op jit(solution)/shard_map/pallas_call | solution.py:393
  99.1 2.0 %shard_map.60 = (bf16[1280,256]{1,0:T(8,128)(2,1)}, f32[1,32,256]{2,1,0:T(8,128)}) custom-call(bf16[1280,256]{1,0:T(8,128)(2,1)} %get-tuple-element.4.cols_ref, f32[1,32,256]{2,1,0:T(8,128)} %get-tuple-element.5.diag_ref), custom_call_target="tpu_custom_call" | custom-call | tf_op jit(solution)/shard_map/pallas_call | solution.py:424

commit v6 on v5

--- a/solution.py
+++ b/solution.py
@@ -9,12 +9,12 @@
 from jax.sharding import PartitionSpec as P
 
 LANES = 128
-PARTS = 2
+PARTS = 4
 TILES = 5
-DELAY = 1
+DELAY = 2
 HOPS = 1
 AHEAD = 1
-EARLY = 1
+EARLY = 2
 MESH = pl.DeviceIdType.MESH
 
 

time: 101 us -> 123 us (1.22)
  Pallas kernels: 100 us -> 122 us
    pallas_call x1, Pallas kernels: 98.5 us -> 121 us  [body(): pl.pallas_call(functools.partial(kernel, R, C, X), out_shape=out_shape, i...]
where the time goes in v6:
time: 123 us
  Pallas kernels  122 us (99%)
    pallas_call x1, Pallas kernels, body(): pl.pallas_call(functools.partial(kernel, R, C, X), out_shape=out_shape, i...  121 us

profile of v6, /device:TPU:1, one launch (start us, length us, event | category | flops | bytes accessed | tf_op | source)
XLA Modules:
  0.0 123.1 jit_solution(8851243802313447516)
XLA Ops:
  0.6 120.5 %shard_map.59 = (bf16[1280,256]{1,0:T(8,128)(2,1)}, f32[1,32,256]{2,1,0:T(8,128)}) custom-call(s32[4,40]{1,0:T(4,128)} %bitcast.1, bf16[1280,256]{1,0:T(8,128)(2,1)} %factor_ref.1, f32[1,32,256]{2,1,0:T(8,128)} %diag_ref.1, bf16[1280,2560]{1,0:T(8,128)(2,1)} %a_hbm.1), custom_call_target="tpu_custom_call" | custom-call | flops 6710886400 | bytes 6553600 | tf_op jit(solution)/shard_map/pallas_call | solution.py:393
  121.1 2.0 %shard_map.60 = (bf16[1280,256]{1,0:T(8,128)(2,1)}, f32[1,32,256]{2,1,0:T(8,128)}) custom-call(bf16[1280,256]{1,0:T(8,128)(2,1)} %get-tuple-element.4.cols_ref, f32[1,32,256]{2,1,0:T(8,128)} %get-tuple-element.5.diag_ref), custom_call_target="tpu_custom_call" | custom-call | tf_op jit(solution)/shard_map/pallas_call | solution.py:424

commit v7 on v5

--- a/solution.py
+++ b/solution.py
@@ -328,20 +328,23 @@
             swapped(j // parts)
             swaps.add(j // parts)
         across(j)
-    jobs, done = [], 0
-    for j in range(J):
+    jobs, done, sent = [], 0, 0
+    for s in range(J + max(Z - 2, 0)):
         for d in range(1, Z):
-            arrivals(j, d)
-            if d == 1 and j + AHEAD < J:
-                own(j + AHEAD)
-            if d == max(Z - 2, 1) and j >= 1:
-                forward(j - 1)
+            if 0 <= s - d + 1 < J:
+                arrivals(s - d + 1, d)
+            if d == 1 and s + AHEAD < J:
+                own(s + AHEAD)
+            if d == max(Z - 2, 1) and s >= Z - 1:
+                forward(s - Z + 1)
+                sent = s - Z + 2
             if jobs:
                 jobs.pop(0)()
-        if j - DELAY >= (done + 1) * parts:
+        if sent - DELAY >= (done + 1) * parts:
             jobs += work(done)
             done += 1
-    forward(J - 1)
+    for j in range(sent, J):
+        forward(j)
     for job in jobs:
         job()
     for q in range(done, Q):

time: 101 us -> 109 us (1.079)
  Pallas kernels: 100 us -> 107 us
    pallas_call x1, Pallas kernels: 98.5 us -> 105 us  [body(): pl.pallas_call(functools.partial(kernel, R, C, X), out_shape=out_shape, i...]
where the time goes in v7:
time: 109 us; the launch traced here: 108 us
  Pallas kernels  107 us (98%)
    pallas_call x1, Pallas kernels, body(): pl.pallas_call(functools.partial(kernel, R, C, X), out_shape=out_shape, i...  105 us

profile of v7, /device:TPU:1, one launch (start us, length us, event | category | flops | bytes accessed | tf_op | source)
XLA Modules:
  0.0 108.1 jit_solution(9857083751527867709)
XLA Ops:
  0.6 105.5 %shard_map.59 = (bf16[1280,256]{1,0:T(8,128)(2,1)}, f32[1,32,256]{2,1,0:T(8,128)}) custom-call(s32[4,40]{1,0:T(4,128)} %bitcast.1, bf16[1280,256]{1,0:T(8,128)(2,1)} %factor_ref.1, f32[1,32,256]{2,1,0:T(8,128)} %diag_ref.1, bf16[1280,2560]{1,0:T(8,128)(2,1)} %a_hbm.1), custom_call_target="tpu_custom_call" | custom-call | flops 6710886400 | bytes 6553600 | tf_op jit(solution)/shard_map/pallas_call | solution.py:396
  106.1 2.0 %shard_map.60 = (bf16[1280,256]{1,0:T(8,128)(2,1)}, f32[1,32,256]{2,1,0:T(8,128)}) custom-call(bf16[1280,256]{1,0:T(8,128)(2,1)} %get-tuple-element.4.cols_ref, f32[1,32,256]{2,1,0:T(8,128)} %get-tuple-element.5.diag_ref), custom_call_target="tpu_custom_call" | custom-call | tf_op jit(solution)/shard_map/pallas_call | solution.py:427

commit v8 on v5

--- a/solution.py
+++ b/solution.py
@@ -14,7 +14,7 @@
 DELAY = 1
 HOPS = 1
 AHEAD = 1
-EARLY = 1
+EARLY = 2
 MESH = pl.DeviceIdType.MESH
 
 

time: 101 us -> 107 us (1.059); the launches traced: 101 us -> 105 us
  Pallas kernels: 100 us -> 105 us
    pallas_call x1, Pallas kernels: 98.5 us -> 103 us  [body(): pl.pallas_call(functools.partial(kernel, R, C, X), out_shape=out_shape, i...]
where the time goes in v8:
time: 107 us; the launch traced here: 105 us
  Pallas kernels  105 us (98%)
    pallas_call x1, Pallas kernels, body(): pl.pallas_call(functools.partial(kernel, R, C, X), out_shape=out_shape, i...  103 us

profile of v8, /device:TPU:1, one launch (start us, length us, event | category | flops | bytes accessed | tf_op | source)
XLA Modules:
  0.0 105.2 jit_solution(16065483381200949572)
XLA Ops:
  0.6 102.6 %shard_map.59 = (bf16[1280,256]{1,0:T(8,128)(2,1)}, f32[1,32,256]{2,1,0:T(8,128)}) custom-call(s32[4,40]{1,0:T(4,128)} %bitcast.1, bf16[1280,256]{1,0:T(8,128)(2,1)} %factor_ref.1, f32[1,32,256]{2,1,0:T(8,128)} %diag_ref.1, bf16[1280,2560]{1,0:T(8,128)(2,1)} %a_hbm.1), custom_call_target="tpu_custom_call" | custom-call | flops 6710886400 | bytes 6553600 | tf_op jit(solution)/shard_map/pallas_call | solution.py:393
  103.2 2.0 %shard_map.60 = (bf16[1280,256]{1,0:T(8,128)(2,1)}, f32[1,32,256]{2,1,0:T(8,128)}) custom-call(bf16[1280,256]{1,0:T(8,128)(2,1)} %get-tuple-element.4.cols_ref, f32[1,32,256]{2,1,0:T(8,128)} %get-tuple-element.5.diag_ref), custom_call_target="tpu_custom_call" | custom-call | tf_op jit(solution)/shard_map/pallas_call | solution.py:424
